TPU v7x, 1024 devices: a whole 4x8x16 slice. The times are simulated.
1024 devices in a mesh: group: 64 (over y, z_lo), local: 16 (over z_hi, x, core).
Axes of the slice: x: 4, y: 8, z: 16 (z_hi: 2, z_lo: 8; z = z_hi * 8 + z_lo), core: 2. Of those that a mesh axis runs over, the one named last changes fastest.
Arguments:
- looked_rows: bfloat16 [1024, 4096, 2, 128], P(('group', 'local')), may hold values from -6 to 6
- lengths: int32 [1024, 4096], P(('group', 'local')), may hold values from 0 to 2
- assign: int32 [64, 16], P('group'), may hold values from 0 to 15, each once within a row
- labels: int32 [4096], P('local'), may hold values 0 or 1
- tower_first: bfloat16 [64, 2048, 512], P('group'), may hold values from -0.125 to 0.125
- bias_first: bfloat16 [64, 512], P('group'), may hold values from -3 to 3
- tower_second: bfloat16 [64, 512, 512], P('group'), may hold values from -0.25 to 0.25
- bias_second: bfloat16 [64, 512], P('group'), may hold values from -3 to 3
- over_weight: bfloat16 [32768, 2048], P('group'), may hold values from -0.03125 to 0.03125
- over_bias: bfloat16 [2048], replicated, may hold values from -3 to 3
- out_weight: bfloat16 [2048], replicated, may hold values from -0.125 to 0.125
Outputs:
- scores: float32 [4096], P(('local', 'group'))
- pooled_grad: bfloat16 [1024, 4096, 128], P(('group', 'local'))
Inputs may be any that keep to these rules, and one draw needn't show every extreme that they name: Each row of assign names each of 0 to 15 once.
All inputs are finite; a program needn't handle non-finite values. No bound on the sum of `labels` on one device may be relied on, other than what follows from the above.
Results may differ from a plain program's by a relative error of at most 0.014.
Values may be sent and summed in bfloat16 or wider, within the bound.
A program may use at most 32 MiB of HBM per device.

v0:
```python
import jax
import jax.numpy as jnp
from jax import lax
from jax.sharding import PartitionSpec as P

loss_scale = 2048.0


def silu_slope(values):
    squash = jax.nn.sigmoid(values)
    return squash * (1.0 + values * (1.0 - squash))


def pool_rows(group_rows, group_lengths):
    running = jnp.zeros(group_rows.shape[:2] + group_rows.shape[3:], jnp.float32)
    for position in range(group_rows.shape[2]):
        live_mask = (group_lengths > position)[..., None]
        running = running + jnp.where(
            live_mask, group_rows[:, :, position, :].astype(jnp.float32), jnp.float32(0.0)
        )
    return running.astype(jnp.bfloat16)


def on_device(
    looked_rows,
    lengths,
    assign,
    labels,
    tower_first,
    bias_first,
    tower_second,
    bias_second,
    over_weight,
    over_bias,
    out_weight,
):
    local_count = lax.axis_size("local")
    group_count = lax.axis_size("group")
    batch_size = looked_rows.shape[1]
    embed_width = looked_rows.shape[3]
    tower_rows = batch_size // local_count
    own_rows = tower_rows // group_count
    pooled = pool_rows(looked_rows, lengths).reshape(local_count, tower_rows, embed_width)
    arrived = lax.all_to_all(pooled, "local", split_axis=0, concat_axis=0, tiled=True)
    picker = (assign[0][:, None] == jnp.arange(local_count, dtype=jnp.int32)[None, :]).astype(
        jnp.bfloat16
    )
    slotted = jnp.einsum("sm,mre->sre", picker, arrived, preferred_element_type=jnp.float32).astype(
        jnp.bfloat16
    )
    first_weight = tower_first[0].reshape(local_count, embed_width, -1)
    first_pre = jnp.einsum(
        "sre,set->rt", slotted, first_weight, preferred_element_type=jnp.float32
    ) + bias_first[0].astype(jnp.float32)
    first_act = jax.nn.silu(first_pre).astype(jnp.bfloat16)
    second_pre = jnp.dot(
        first_act, tower_second[0], preferred_element_type=jnp.float32
    ) + bias_second[0].astype(jnp.float32)
    tower_out = jax.nn.silu(second_pre).astype(jnp.bfloat16)
    head_bias = over_bias.astype(jnp.float32)
    head_out = out_weight.astype(jnp.float32)
    head_pre = (
        lax.psum_scatter(
            jnp.dot(tower_out, over_weight, preferred_element_type=jnp.float32),
            "group",
            scatter_dimension=0,
            tiled=True,
        )
        + head_bias
    )
    scores = jnp.sum(jax.nn.silu(head_pre) * head_out, axis=1)
    own_labels = lax.dynamic_slice_in_dim(labels, lax.axis_index("group") * own_rows, own_rows, 0)
    seed_grad = loss_scale * (jax.nn.sigmoid(scores) - own_labels.astype(jnp.float32))
    head_grad = (seed_grad[:, None] * head_out * silu_slope(head_pre)).astype(jnp.bfloat16)
    tower_grad = jnp.dot(
        lax.all_gather(head_grad, "group", axis=0, tiled=True),
        over_weight.T,
        preferred_element_type=jnp.float32,
    )
    second_grad = (tower_grad * silu_slope(second_pre)).astype(jnp.bfloat16)
    first_grad = (
        jnp.dot(second_grad, tower_second[0].T, preferred_element_type=jnp.float32)
        * silu_slope(first_pre)
    ).astype(jnp.bfloat16)
    input_grad = jnp.einsum(
        "rt,set->sre", first_grad, first_weight, preferred_element_type=jnp.float32
    ).astype(jnp.bfloat16)
    to_source = jnp.einsum(
        "sm,sre->mre", picker, input_grad, preferred_element_type=jnp.float32
    ).astype(jnp.bfloat16)
    returned = lax.all_to_all(to_source, "local", split_axis=0, concat_axis=0, tiled=True)
    return (scores, returned.reshape(1, batch_size, embed_width))


def solution(mesh):
    return jax.shard_map(
        on_device,
        mesh=mesh,
        in_specs=(
            P(("group", "local"), None, None, None),
            P(("group", "local"), None),
            P("group", None),
            P("local"),
            P("group", None, None),
            P("group", None),
            P("group", None, None),
            P("group", None),
            P("group", None),
            P(),
            P(),
        ),
        out_specs=(P(("local", "group")), P(("group", "local"), None, None)),
        check_vma=False,
    )
```

profile of v0, /device:TPU:1, one launch (start us, length us, event | category | flops | bytes accessed | tf_op | source)
XLA Modules:
  0.0 1496.7 jit_solution(1599276659204580917)
XLA Ops:
  7.2 5.7 fusion.30
  12.8 0.1 copy.39
  13.0 1.1 copy.40
  14.1 0.1 compare_reduce_fusion.1
  14.3 4.0 fusion.1
  18.3 22.7 %all-to-all-start = ((bf16[16,256,128]{2,1,0:T(8,128)(2,1)}), bf16[16,256,128]{2,1,0:T(8,128)(2,1)S(1)}, u32[]{:S(2)}, u32[]{:S(2)}) async-start(bf16[16,256,128]{2,1,0:T(8,128)(2,1)} %fusion.1), calls=%async_computation | async-start | bytes 2097152 | tf_op jit(solution)/shard_map/all_to_all | solution.py:44
  41.0 0.0 all-reduce.3.cloned.1.call-start
  41.1 26.3 %all-to-all-done = bf16[16,256,128]{2,1,0:T(8,128)(2,1)S(1)} async-done(((bf16[16,256,128]{2,1,0:T(8,128)(2,1)}), bf16[16,256,128]{2,1,0:T(8,128)(2,1)S(1)}, u32[]{:S(2)}, u32[]{:S(2)}) %all-to-all-start) | async-done | bytes 1048608 | tf_op jit(solution)/shard_map/all_to_all | solution.py:44
  67.4 0.8 convolution_convert_fusion.2
  68.2 0.7 fusion.3
  68.9 0.3 copy-done.10
  69.2 0.3 convolution_add_fusion
  69.6 0.2 copy-done.12
  69.7 0.8 copy-done.11
  70.5 0.3 copy-done.9
  70.8 2.1 fusion.16
  72.9 0.0 all-gather.3.cloned.1.call-start
  72.9 0.6 copy-done.2
  73.6 1.3 dynamic-slice
  75.5 878.4 %all-reduce.3.cloned.1.call-done = f32[256,2048]{1,0:T(8,128)} async-done(((f32[256,2048]{1,0:T(8,128)}), f32[256,2048]{1,0:T(8,128)}) %all-reduce.3.cloned.1.call-update) | async-done | bytes 2097168
  953.9 1.0 multiply_reduce_fusion
  954.9 0.1 fusion.26
  955.0 1.5 fusion.20
  956.5 0.0 all-gather.3.cloned.1.call-update
  956.6 431.6 %all-gather.3.cloned.1.call-done = bf16[64,4,2048]{2,1,0:T(4,128)(2,1)} async-done(((bf16[1,4,2048]{2,1,0:T(4,128)(2,1)}), bf16[64,4,2048]{2,1,0:T(4,128)(2,1)}) %all-gather.3.cloned.1.call-update) | async-done | bytes 1048592 | tf_op jit(solution)/shard_map/all_gather | solution.py:76
  1388.2 1.3 reshape.52
  1389.5 3.2 fusion.6
  1392.7 0.7 fusion.2
  1393.5 0.7 convolution_convert_fusion.1
  1394.2 0.3 copy.36
  1394.5 94.4 %all_to_all.10 = bf16[16,256,128]{2,1,0:T(8,128)(2,1)S(1)} all-to-all(bf16[16,256,128]{2,1,0:T(8,128)(2,1)S(1)} %copy.36), channel_id=1, replica_groups=mesh['group'=64,'local'=16] {'local'}, dimensions={0} | all-to-all | bytes 2097152 | tf_op jit(solution)/shard_map/all_to_all | solution.py:91
  1488.9 1.0 copy.49
  (28 shorter events, 0.1 us)
Async XLA Ops:
  7.2 61.0 %copy-start = (bf16[1,2048,512]{2,1,0:T(8,128)(2,1)S(1)}, bf16[1,2048,512]{2,1,0:T(8,128)(2,1)}, u32[]{:S(2)}) copy-start(bf16[1,2048,512]{2,1,0:T(8,128)(2,1)} %param.15) | copy-start | bytes 6291460
  13.0 1.1 copy-start.1
  14.2 26.8 %copy-start.6 = (bf16[1,512]{1,0:T(2,128)(2,1)S(1)}, bf16[1,512]{1,0:T(2,128)(2,1)}, u32[]{:S(2)}) copy-start(bf16[1,512]{1,0:T(2,128)(2,1)} %param.16) | copy-start | bytes 3076
  14.3 26.8 %copy-start.7 = (bf16[1,512]{1,0:T(2,128)(2,1)S(1)}, bf16[1,512]{1,0:T(2,128)(2,1)}, u32[]{:S(2)}) copy-start(bf16[1,512]{1,0:T(2,128)(2,1)} %param.18) | copy-start | bytes 3076
  14.3 53.1 %copy-start.4 = (s32[1,16]{1,0:T(1,128)S(1)}, s32[1,16]{1,0:T(1,128)}, u32[]{:S(2)}) copy-start(s32[1,16]{1,0:T(1,128)} %param.13) | copy-start | bytes 196
  18.3 49.1 %all-to-all-start = ((bf16[16,256,128]{2,1,0:T(8,128)(2,1)}), bf16[16,256,128]{2,1,0:T(8,128)(2,1)S(1)}, u32[]{:S(2)}, u32[]{:S(2)}) async-start(bf16[16,256,128]{2,1,0:T(8,128)(2,1)} %fusion.1), calls=%async_computation | async-start | bytes 2097152 | tf_op jit(solution)/shard_map/all_to_all | solution.py:44
  41.0 912.9 %all-reduce.3.cloned.1.call-start = ((), (), s32[]{:S(2)}) async-start(), calls=%async_computation.3 | async-start | bytes 4194304
  68.2 1.0 copy-start.10
  68.9 0.8 copy-start.12
  68.9 1.9 copy-start.9
  69.7 0.8 copy-start.11
  72.8 0.7 copy-start.2
  72.9 0.7 copy-start.3
  72.9 882.1 %copy-start.8 = (s32[256]{0:T(256)S(1)}, s32[256]{0:T(256)}, u32[]{:S(2)}) copy-start(s32[256]{0:T(256)} %param.14) | copy-start | bytes 3076
  72.9 1315.3 %all-gather.3.cloned.1.call-start = ((), (), s32[]{:S(2)}) async-start(), calls=%async_computation.2 | async-start | bytes 1064960 | tf_op jit(solution)/shard_map/all_gather | solution.py:76
  954.9 437.8 %copy-start.5 = (f32[4]{0:T(128)}, f32[4]{0:T(128)S(1)}, u32[]{:S(2)}) copy-start(f32[4]{0:T(128)S(1)} %multiply_reduce_fusion) | copy-start | bytes 52
Sparse Core Ops, SparseCore 0:
  73.0 880.8 all-reduce.2
  956.9 431.2 all-gather.2
where the time goes:
time: 1500 us
  waiting for transfers between devices  1340 us (89%)
  blocking collectives  94.4 us (6%)
  starting transfers between devices  22.8 us (2%)
    unnamed x3, waiting for transfers between devices  878 us
    all_gather x1, waiting for transfers between devices, on_device(): lax.all_gather(head_grad, 'group', axis=0, tiled=True)  432 us
    all_to_all x1, blocking collectives, on_device(): lax.all_to_all(to_source, 'local', split_axis=0, concat_axis=0, tiled=True)  94.4 us
  transfers between devices with their start and end apart: 3, of which 3 were waited for; matrix products, arithmetic and copies ran while one was open for 0% of the time, Pallas kernels for 0%

commit v1 on v0

v1 whole, which is shorter than its diff:
```python
import functools

import jax
import jax.numpy as jnp
from jax import lax
from jax.experimental import pallas as pl
from jax.experimental.pallas import tpu as pltpu
from jax.sharding import PartitionSpec as P

MESH = pl.DeviceIdType.MESH
loss_scale = 2048.0

N = 8
CHUNKS = 4
ROWS = N * N
E = 128
TW = 512
H = 2048
SLOTS = 16
UNIT = 128
LAG = dict(tower=0, gather=2, loss=3, spread=4, back=6, rows=8)


def silu_slope(values):
    squash = jax.nn.sigmoid(values)
    return squash * (1.0 + values * (1.0 - squash))


def silu(values):
    return values * jax.nn.sigmoid(values)


def dot(a, b):
    return jnp.dot(a, b, preferred_element_type=jnp.float32)


def dot_t(a, b):
    return lax.dot_general(a, b, (((1,), (1,)), ((), ())), preferred_element_type=jnp.float32)


def kernel(
    looked_hbm,
    lengths_hbm,
    assign_hbm,
    labels_hbm,
    first_hbm,
    bias_first_hbm,
    second_hbm,
    bias_second_hbm,
    over_hbm,
    over_bias_hbm,
    out_weight_hbm,
    scores_ref,
    grad_hbm,
    assign_ref,
    labels_ref,
    bias_first_ref,
    bias_second_ref,
    over_bias_ref,
    out_weight_ref,
    looked,
    lengths,
    first,
    second,
    over,
    slots,
    pooled,
    arrived,
    part_out,
    part_in,
    first_pre,
    second_pre,
    head_out,
    head_in,
    turn,
    row_out,
    row_in,
    mine_grad,
    line_grad,
    share_grad,
    full_grad,
    own_first_grad,
    far_first_grad,
    table_grad,
    score_out,
    score_in,
    load_sem,
    send_sem,
    arrived_sem,
    part_sem,
    head_sem,
    row_sem,
    line_sem,
    full_sem,
    far_sem,
    grad_sem,
    score_sem,
    score_send_sem,
):
    group = lax.axis_index("group")
    local = lax.axis_index("local")
    y, zl = lax.div(group, N), lax.rem(group, N)
    half, col = lax.div(local, N), lax.rem(local, N)
    other_half = 1 - half

    def turned(at, by):
        return lax.rem(at + by, N)

    def col_peer(d):
        return (group, half * N + turned(col, d))

    def y_peer(d):
        return (turned(y, d) * N + zl, local)

    def z_peer(d):
        return (y * N + turned(zl, d), local)

    far = (group, other_half * N + col)

    def remote(src, dst, ss, rs, to):
        pltpu.make_async_remote_copy(
            src_ref=src, dst_ref=dst, send_sem=ss, recv_sem=rs, device_id=to, device_id_type=MESH
        ).start()

    def wait(ref, sem):
        pltpu.make_async_copy(ref, ref, sem).wait()

    def score_source(i):
        return lax.rem(CHUNKS * group + i, ROWS)

    def score_target(k):
        return lax.div(ROWS * k + group, CHUNKS)

    barrier = pltpu.get_barrier_semaphore()
    for d in range(1, N):
        for peer in (col_peer(d), y_peer(d), z_peer(d)):
            pl.semaphore_signal(barrier, inc=1, device_id=peer, device_id_type=MESH)
    pl.semaphore_signal(barrier, inc=1, device_id=far, device_id_type=MESH)
    for i in range(CHUNKS):

        @pl.when(score_source(i) != group)
        def _():
            pl.semaphore_signal(
                barrier, inc=1, device_id=(score_source(i), local), device_id_type=MESH
            )

    loads = [
        pltpu.make_async_copy(src, dst, load_sem.at[i])
        for i, (src, dst) in enumerate(
            (
                (lengths_hbm, lengths),
                (looked_hbm, looked),
                (assign_hbm, assign_ref),
                (labels_hbm, labels_ref),
                (first_hbm, first),
                (bias_first_hbm, bias_first_ref),
                (second_hbm, second),
                (bias_second_hbm, bias_second_ref),
                (over_hbm, over),
                (over_bias_hbm, over_bias_ref),
                (out_weight_hbm, out_weight_ref),
            )
        )
    ]
    for load in loads:
        load.start()

    def pool_units(parity):
        def pool_unit(block, carry):
            unit = 2 * block + parity
            live = lengths[pl.ds(unit, 1), :]
            row = lax.broadcasted_iota(jnp.int32, (2 * UNIT, UNIT), 0)
            sample = lax.broadcasted_iota(jnp.int32, (2 * UNIT, UNIT), 1)
            place = row - 2 * sample
            mask = jnp.where((place >= 0) & (place < live), 1.0, 0.0).astype(jnp.bfloat16)
            rows = looked[pl.ds(pl.multiple_of(unit * 2 * UNIT, 2 * UNIT), 2 * UNIT), :]
            total = lax.dot_general(
                mask, rows, (((0,), (0,)), ((), ())), preferred_element_type=jnp.float32
            ).astype(jnp.bfloat16)
            for q in range(UNIT // ROWS):
                pooled[lax.rem(block, N), parity * (UNIT // ROWS) + q, lax.div(block, N)] = total[
                    q * ROWS : (q + 1) * ROWS
                ]
            return carry

        lax.fori_loop(0, 2 * N, pool_unit, 0)

    def send_pooled(k):
        for d in range(1, N):
            to = turned(col, d)
            remote(
                pooled.at[to, k],
                arrived.at[k, col],
                send_sem.at[0],
                arrived_sem.at[k],
                (group, half * N + to),
            )
        pltpu.make_async_copy(pooled.at[col, k], arrived.at[k, col], arrived_sem.at[k]).start()

    loads[0].wait()
    loads[1].wait()
    pool_units(0)
    to_come = 3 * (N - 1) + 1
    for k in range(CHUNKS):
        to_come = to_come + jnp.where(score_target(k) != group, 1, 0)
    pl.semaphore_wait(barrier, to_come)
    send_pooled(0)
    send_pooled(1)
    pool_units(1)
    send_pooled(2)
    send_pooled(3)
    for load in loads[2:]:
        load.wait()

    for m in range(N):
        slot = jnp.int32(0)
        for s in range(SLOTS):
            slot = jnp.maximum(slot, jnp.where(assign_ref[0, s] == half * N + m, s, 0))
        slots[m] = slot

    def half_first(k, which):
        total = jnp.zeros((ROWS, TW), jnp.float32)
        for m in range(0, N, 2):
            rows = jnp.concatenate([arrived[k, m, which], arrived[k, m + 1, which]], axis=1)
            weight = jnp.concatenate([first[slots[m]], first[slots[m + 1]]], axis=0)
            total = total + dot(rows, weight)
        return total

    def partial_stage(k):
        wait(arrived.at[k], arrived_sem.at[k])
        part_out[k] = half_first(k, other_half).astype(jnp.bfloat16)
        remote(part_out.at[k], part_in.at[k], send_sem.at[1], part_sem.at[k], far)
        first_pre[k] = half_first(k, half) + bias_first_ref[...].astype(jnp.float32)

    def tower_stage(k):
        wait(part_in.at[k], part_sem.at[k])
        pre = first_pre[k] + part_in[k].astype(jnp.float32)
        first_pre[k] = pre
        act = silu(pre).astype(jnp.bfloat16)
        pre = dot(act, second[...]) + bias_second_ref[...].astype(jnp.float32)
        second_pre[k] = pre
        out = silu(pre).astype(jnp.bfloat16)
        for c in range(2):
            low = dot(out, over[:, c * 512 : (c + 1) * 512])
            high = dot(out, over[:, 1024 + c * 512 : 1024 + (c + 1) * 512])
            for v in range(N):
                head_out[k, v, :, c * 512 : (c + 1) * 512] = jnp.concatenate(
                    [low[v * N : (v + 1) * N], high[v * N : (v + 1) * N]], axis=0
                ).astype(jnp.bfloat16)
        for d in range(1, N):
            to = turned(y, d)
            remote(
                head_out.at[k, to],
                head_in.at[k, y],
                send_sem.at[2],
                head_sem.at[k],
                (to * N + zl, local),
            )
        pltpu.make_async_copy(head_out.at[k, y], head_in.at[k, y], head_sem.at[k]).start()

    def gather_stage(k):
        wait(head_in.at[k], head_sem.at[k])
        total = head_in[k, 0].astype(jnp.float32)
        for v in range(1, N):
            total = total + head_in[k, v].astype(jnp.float32)
        for s in range(2):
            for t in range(N):
                turn[pl.ds((s * N + t) * N, N), :] = total[
                    s * N : (s + 1) * N, t * 128 : (t + 1) * 128
                ]
        for v in range(N):
            row_out[k, v] = jnp.concatenate(
                [turn[pl.ds(s * N * N + v, N, stride=N), :] for s in range(2)], axis=0
            ).astype(jnp.bfloat16)
        for d in range(1, N):
            to = turned(zl, d)
            remote(
                row_out.at[k, to],
                row_in.at[k, zl],
                send_sem.at[3],
                row_sem.at[k],
                (y * N + to, local),
            )
        pltpu.make_async_copy(row_out.at[k, zl], row_in.at[k, zl], row_sem.at[k]).start()

    def loss_stage(k):
        wait(row_in.at[k], row_sem.at[k])
        pre = over_bias_ref[...].astype(jnp.float32)
        for v in range(N):
            pre = pre + row_in[k, v].astype(jnp.float32)
        weight = out_weight_ref[...].astype(jnp.float32)
        score = jnp.sum(
            jnp.sum(silu(pre) * weight, axis=0, keepdims=True), axis=1, keepdims=True
        )
        label = labels_ref[ROWS * k + group].astype(jnp.float32)
        seed = loss_scale * (jax.nn.sigmoid(score) - label)
        mine_grad[k] = (seed * weight * silu_slope(pre)).astype(jnp.bfloat16)
        for d in range(1, N):
            remote(mine_grad.at[k], line_grad.at[k, zl], send_sem.at[4], line_sem.at[k], z_peer(d))
        pltpu.make_async_copy(mine_grad.at[k], line_grad.at[k, zl], line_sem.at[k]).start()
        score_out[k] = jnp.broadcast_to(score, (8, 128))
        target = score_target(k)
        place = lax.rem(group, CHUNKS)

        @pl.when(target != group)
        def _():
            remote(
                score_out.at[k],
                score_in.at[place],
                score_send_sem.at[k],
                score_sem.at[0],
                (target, local),
            )

        @pl.when(target == group)
        def _():
            pltpu.make_async_copy(score_out.at[k], score_in.at[place], score_sem.at[0]).start()

    def spread_stage(k):
        wait(line_grad.at[k], line_sem.at[k])
        for v in range(N):
            turn[pl.ds(v * 2 * N, 2 * N), :] = line_grad[k, v].astype(jnp.float32)
        for t in range(N):
            share_grad[k, :, t * 128 : (t + 1) * 128] = jnp.concatenate(
                [turn[pl.ds(s * N + t, N, stride=2 * N), :] for s in range(2)], axis=0
            ).astype(jnp.bfloat16)
        for d in range(1, N):
            remote(share_grad.at[k], full_grad.at[k, y], send_sem.at[5], full_sem.at[k], y_peer(d))
        pltpu.make_async_copy(share_grad.at[k], full_grad.at[k, y], full_sem.at[k]).start()

    def back_stage(k):
        wait(full_grad.at[k], full_sem.at[k])
        rows = full_grad[k].reshape(2 * ROWS, H // 2)
        low = dot_t(rows, over[:, : H // 2])
        high = dot_t(rows, over[:, H // 2 :])
        tower_grad = jnp.concatenate(
            [
                low[v * 2 * N : v * 2 * N + N] + high[v * 2 * N + N : (v + 1) * 2 * N]
                for v in range(N)
            ],
            axis=0,
        )
        second_grad = (tower_grad * silu_slope(second_pre[k])).astype(jnp.bfloat16)
        own_first_grad[k] = (
            dot_t(second_grad, second[...]) * silu_slope(first_pre[k])
        ).astype(jnp.bfloat16)
        remote(own_first_grad.at[k], far_first_grad.at[k], send_sem.at[6], far_sem.at[k], far)
        half_rows(k, own_first_grad[k], half)

    def half_rows(k, grad, which):
        for m in range(0, N, 2):
            weight = jnp.concatenate([first[slots[m]], first[slots[m + 1]]], axis=0)
            out = dot_t(grad, weight).astype(jnp.bfloat16)
            table_grad[k, m, which] = out[:, :E]
            table_grad[k, m + 1, which] = out[:, E:]

    def rows_stage(k):
        wait(far_first_grad.at[k], far_sem.at[k])
        half_rows(k, far_first_grad[k], other_half)
        span = pl.ds(pl.multiple_of(k * ROWS, ROWS), ROWS)
        for d in range(1, N):
            to = turned(col, d)
            remote(
                table_grad.at[k, to],
                grad_hbm.at[:, col, span],
                send_sem.at[7],
                grad_sem.at[0],
                (group, half * N + to),
            )
        pltpu.make_async_copy(
            table_grad.at[k, col], grad_hbm.at[:, col, span], grad_sem.at[0]
        ).start()

    def partials(k, carry):
        partial_stage(k)
        return carry

    lax.fori_loop(0, CHUNKS, partials, 0)

    stages = (
        (tower_stage, LAG["tower"]),
        (gather_stage, LAG["gather"]),
        (loss_stage, LAG["loss"]),
        (spread_stage, LAG["spread"]),
        (back_stage, LAG["back"]),
        (rows_stage, LAG["rows"]),
    )

    def tick(t, carry):
        for stage, lag in stages:

            @pl.when((t >= lag) & (t < lag + CHUNKS))
            def _():
                stage(t - lag)

        return carry

    lax.fori_loop(0, CHUNKS + LAG["rows"], tick, 0)

    wait(score_in, score_sem.at[0])
    lane = lax.broadcasted_iota(jnp.int32, (8, 128), 1)
    packed = jnp.zeros((8, 128), jnp.float32)
    for i in range(CHUNKS):
        packed = packed + jnp.where(lane == i, score_in[i], 0.0)
    scores_ref[...] = packed

    wait(pooled.at[pl.ds(0, N - 1)], send_sem.at[0])
    wait(part_out, send_sem.at[1])
    wait(head_out.at[:, pl.ds(0, N - 1)], send_sem.at[2])
    wait(row_out.at[:, pl.ds(0, N - 1)], send_sem.at[3])
    wait(line_grad.at[:, pl.ds(0, N - 1)], send_sem.at[4])
    wait(full_grad.at[:, pl.ds(0, N - 1)], send_sem.at[5])
    wait(own_first_grad, send_sem.at[6])
    wait(table_grad.at[:, pl.ds(0, N - 1)], send_sem.at[7])
    for k in range(CHUNKS):

        @pl.when(score_target(k) != group)
        def _():
            wait(score_out.at[k], score_send_sem.at[k])

    wait(table_grad, grad_sem.at[0])


def on_device(
    looked_rows,
    lengths,
    assign,
    labels,
    tower_first,
    bias_first,
    tower_second,
    bias_second,
    over_weight,
    over_bias,
    out_weight,
):
    batch = looked_rows.shape[1]
    block = batch // (2 * N)
    bf16, f32 = jnp.bfloat16, jnp.float32
    any_spec = pl.BlockSpec(memory_space=pl.ANY)
    vmem_spec = pl.BlockSpec(memory_space=pltpu.VMEM)
    dma = pltpu.SemaphoreType.DMA
    scores, grad = pl.pallas_call(
        kernel,
        name="tower_step",
        out_shape=(
            jax.ShapeDtypeStruct((8, 128), f32),
            jax.ShapeDtypeStruct((2, N, block, E), bf16),
        ),
        in_specs=[any_spec] * 11,
        out_specs=(vmem_spec, any_spec),
        scratch_shapes=[
            pltpu.SMEM(assign.shape, jnp.int32),
            pltpu.SMEM(labels.shape, jnp.int32),
            pltpu.VMEM(bias_first.shape, bf16),
            pltpu.VMEM(bias_second.shape, bf16),
            pltpu.VMEM((H // 128, 128), bf16),
            pltpu.VMEM((H // 128, 128), bf16),
            pltpu.VMEM((2 * batch, E), bf16),
            pltpu.VMEM((batch // UNIT, UNIT), jnp.int32),
            pltpu.VMEM((SLOTS, E, TW), bf16),
            pltpu.VMEM((TW, TW), bf16),
            pltpu.VMEM((TW, H), bf16),
            pltpu.SMEM((N,), jnp.int32),
            pltpu.VMEM((N, CHUNKS, 2, ROWS, E), bf16),
            pltpu.VMEM((CHUNKS, N, 2, ROWS, E), bf16),
            pltpu.VMEM((CHUNKS, ROWS, TW), bf16),
            pltpu.VMEM((CHUNKS, ROWS, TW), bf16),
            pltpu.VMEM((CHUNKS, ROWS, TW), f32),
            pltpu.VMEM((CHUNKS, ROWS, TW), f32),
            pltpu.VMEM((CHUNKS, N, 2 * N, H // 2), bf16),
            pltpu.VMEM((CHUNKS, N, 2 * N, H // 2), bf16),
            pltpu.VMEM((2 * N * N, 128), f32),
            pltpu.VMEM((CHUNKS, N, 2 * N, 128), bf16),
            pltpu.VMEM((CHUNKS, N, 2 * N, 128), bf16),
            pltpu.VMEM((CHUNKS, 2 * N, 128), bf16),
            pltpu.VMEM((CHUNKS, N, 2 * N, 128), bf16),
            pltpu.VMEM((CHUNKS, 2 * N, H // 2), bf16),
            pltpu.VMEM((CHUNKS, N, 2 * N, H // 2), bf16),
            pltpu.VMEM((CHUNKS, ROWS, TW), bf16),
            pltpu.VMEM((CHUNKS, ROWS, TW), bf16),
            pltpu.VMEM((CHUNKS, N, 2, ROWS, E), bf16),
            pltpu.VMEM((CHUNKS, 8, 128), f32),
            pltpu.VMEM((CHUNKS, 8, 128), f32),
            dma((11,)),
            dma((8,)),
            dma((CHUNKS,)),
            dma((CHUNKS,)),
            dma((CHUNKS,)),
            dma((CHUNKS,)),
            dma((CHUNKS,)),
            dma((CHUNKS,)),
            dma((CHUNKS,)),
            dma((1,)),
            dma((1,)),
            dma((CHUNKS,)),
        ],
        compiler_params=pltpu.CompilerParams(
            collective_id=0, has_side_effects=True, vmem_limit_bytes=63 * 2**20
        ),
    )(
        looked_rows.reshape(2 * batch, E),
        lengths.reshape(batch // UNIT, UNIT),
        assign,
        labels,
        tower_first.reshape(SLOTS, E, TW),
        bias_first,
        tower_second[0],
        bias_second,
        over_weight,
        over_bias.reshape(H // 128, 128),
        out_weight.reshape(H // 128, 128),
    )
    return scores[0, :CHUNKS], grad.reshape(1, batch, E)


def solution(mesh):
    return jax.shard_map(
        on_device,
        mesh=mesh,
        in_specs=(
            P(("group", "local"), None, None, None),
            P(("group", "local"), None),
            P("group", None),
            P("local"),
            P("group", None, None),
            P("group", None),
            P("group", None, None),
            P("group", None),
            P("group", None),
            P(),
            P(),
        ),
        out_specs=(P(("local", "group")), P(("group", "local"), None, None)),
        check_vma=False,
    )
```

time: 1500 us -> 128 us (0.09)
  waiting for transfers between devices: 1340 us -> 0 us
  Pallas kernels: 0 us -> 122 us
  blocking collectives: 94.4 us -> 0 us
  starting transfers between devices: 22.8 us -> 0 us
    unnamed x3 -> x0, waiting for transfers between devices: 878 us -> none
    all_gather x1 -> x0, waiting for transfers between devices: 432 us -> none  [on_device(): lax.all_gather(head_grad, 'group', axis=0, tiled=True)]
    pallas_call x0 -> x1, Pallas kernels: none -> 122 us  [on_device(): pl.pallas_call(kernel, name='tower_step', out_shape=(jax.ShapeDtypeStruct...]
    all_to_all x1 -> x0, blocking collectives: 94.4 us -> none  [on_device(): lax.all_to_all(to_source, 'local', split_axis=0, concat_axis=0, tiled=True)]
    all_to_all x1 -> x0, waiting for transfers between devices: 26.3 us -> none  [on_device(): lax.all_to_all(pooled, 'local', split_axis=0, concat_axis=0, tiled=True)]
    all_to_all x1 -> x0, starting transfers between devices: 22.7 us -> none  [on_device(): lax.all_to_all(pooled, 'local', split_axis=0, concat_axis=0, tiled=True)]
  transfers between devices with their start and end apart: 3 -> 0, of which waited for: 3 -> 0; matrix products, arithmetic and copies ran while one was open for 0% -> 0% of each run, Pallas kernels for 0% -> 0%
where the time goes in v1:
time: 128 us; the launch traced here: 126 us
  Pallas kernels  122 us (95%)
  local copies, waits for them, and re-layouts  3.45 us (3%)
    pallas_call x1, Pallas kernels, on_device(): pl.pallas_call(kernel, name='tower_step', out_shape=(jax.ShapeDtypeStruct...  122 us

profile of v1, /device:TPU:1, one launch (start us, length us, event | category | flops | bytes accessed | tf_op | source)
XLA Modules:
  0.0 126.3 jit_solution(13040173016987146074)
XLA Ops:
  0.6 122.2 %tower_step.1 = (f32[8,128]{1,0:T(8,128)}, bf16[2,8,256,128]{3,2,1,0:T(8,128)(2,1)}) custom-call(bf16[8192,128]{1,0:T(8,128)(2,1)} %bitcast.9, s32[32,128]{1,0:T(8,128)} %bitcast.13, s32[1,16]{1,0:T(1,128)} %assign_hbm.1, s32[256]{0:T(256)} %labels_hbm.1, bf16[16,128,512]{2,1,0:T(8,128)(2,1)} %bitcast.10, bf16[1,512]{1,0:T(2,128)(2,1)} %bias_first_hbm.1, ...), custom_call_target="tpu_custom_call" | custom-call | tf_op jit(solution)/shard_map/tower_step/pallas_call | solution.py:443
  122.8 1.2 slice_bitcast_fusion
  124.0 2.3 %copy.14 = bf16[1,4096,128]{2,1,0:T(8,128)(2,1)} copy(bf16[1,4096,128]{2,1,0:T(8,128)(2,1)} %bitcast.11) | data formatting | bytes 2097152

commit v2 on v1

v2 whole, which is shorter than its diff:
```python
import functools

import jax
import jax.numpy as jnp
from jax import lax
from jax.experimental import pallas as pl
from jax.experimental.pallas import tpu as pltpu
from jax.sharding import PartitionSpec as P

MESH = pl.DeviceIdType.MESH
loss_scale = 2048.0

N = 8
OWN = 4
PAIRS = 4
WIDE = 64
CHUNKS = 2 * PAIRS
ROWS = WIDE // 2
SHARE = ROWS // N
EARLY = 2
QUARTER = 512
E = 128
TW = 512
H = 2048
SLOTS = 16
UNIT = 128
LAST = 20


def silu_slope(values):
    squash = jax.nn.sigmoid(values)
    return squash * (1.0 + values * (1.0 - squash))


def silu(values):
    return values * jax.nn.sigmoid(values)


def dot(a, b):
    return jnp.dot(a, b, preferred_element_type=jnp.float32)


def dot_t(a, b):
    return lax.dot_general(a, b, (((1,), (1,)), ((), ())), preferred_element_type=jnp.float32)


def kernel(
    looked_hbm,
    lengths_hbm,
    assign_hbm,
    labels_hbm,
    first_hbm,
    bias_first_hbm,
    second_hbm,
    bias_second_hbm,
    over_hbm,
    over_bias_hbm,
    out_weight_hbm,
    scores_ref,
    grad_hbm,
    assign_ref,
    labels_ref,
    bias_first_ref,
    bias_second_ref,
    over_bias_ref,
    out_weight_ref,
    looked,
    lengths,
    live,
    first,
    second,
    over,
    slots,
    pooled,
    arrived,
    part_out,
    part_in,
    first_pre,
    second_pre,
    head_out,
    head_in,
    turn,
    bias_turned,
    weight_turned,
    row_out,
    row_in,
    mine_grad,
    line_grad,
    share_grad,
    full_grad,
    own_first_grad,
    far_first_grad,
    table_grad,
    score_out,
    score_in,
    load_sem,
    send_sem,
    arrived_sem,
    part_sem,
    head_sem,
    row_sem,
    line_sem,
    full_sem,
    far_sem,
    grad_sem,
    score_sem,
    score_send_sem,
    part_send_sem,
):
    group = lax.axis_index("group")
    local = lax.axis_index("local")
    y, zl = lax.div(group, N), lax.rem(group, N)
    half, col = lax.div(local, N), lax.rem(local, N)
    other_half = 1 - half

    def turned(at, by):
        return lax.rem(at + by, N)

    def col_peer(d):
        return (group, half * N + turned(col, d))

    def y_peer(d):
        return (turned(y, d) * N + zl, local)

    def z_peer(d):
        return (y * N + turned(zl, d), local)

    far = (group, other_half * N + col)

    def remote(src, dst, ss, rs, to):
        pltpu.make_async_remote_copy(
            src_ref=src, dst_ref=dst, send_sem=ss, recv_sem=rs, device_id=to, device_id_type=MESH
        ).start()

    def wait(ref, sem):
        pltpu.make_async_copy(ref, ref, sem).wait()

    side, lane_row = lax.div(zl, SHARE), lax.rem(zl, SHARE)

    def score_source(i):
        return zl * N + SHARE * lax.rem(y, 2) + i

    def score_target(e):
        return (2 * e + side) * N + y

    barrier = pltpu.get_barrier_semaphore()
    for d in range(1, N):
        for peer in (col_peer(d), y_peer(d), z_peer(d)):
            pl.semaphore_signal(barrier, inc=1, device_id=peer, device_id_type=MESH)
    pl.semaphore_signal(barrier, inc=1, device_id=far, device_id_type=MESH)
    for i in range(OWN):

        @pl.when(score_source(i) != group)
        def _():
            pl.semaphore_signal(
                barrier, inc=1, device_id=(score_source(i), local), device_id_type=MESH
            )

    loads = [
        pltpu.make_async_copy(src, dst, load_sem.at[i])
        for i, (src, dst) in enumerate(
            (
                (lengths_hbm, lengths),
                (looked_hbm, looked),
                (assign_hbm, assign_ref),
                (labels_hbm, labels_ref),
                (first_hbm, first),
                (bias_first_hbm, bias_first_ref),
                (second_hbm, second),
                (bias_second_hbm, bias_second_ref),
                (over_hbm, over),
                (over_bias_hbm, over_bias_ref),
                (out_weight_hbm, out_weight_ref),
            )
        )
    ]
    for load in loads:
        load.start()

    def pool_units(parity):
        def pool_unit(block, carry):
            unit = 2 * block + parity
            rows = looked[pl.ds(pl.multiple_of(unit * 2 * UNIT, 2 * UNIT), 2 * UNIT), :]
            mask = jnp.where(pair, live[pl.ds(unit, 1), :], 0.0).astype(jnp.bfloat16)
            total = dot(mask, rows).astype(jnp.bfloat16)
            for q in range(UNIT // WIDE):
                pooled[lax.rem(block, N), parity * (UNIT // WIDE) + q, lax.div(block, N)] = total[
                    q * WIDE : (q + 1) * WIDE
                ]
            return carry

        lax.fori_loop(0, 2 * N, pool_unit, 0, unroll=8)

    def send_pooled(k):
        for d in range(1, N):
            to = turned(col, d)
            remote(
                pooled.at[to, k],
                arrived.at[k, col],
                send_sem.at[0],
                arrived_sem.at[k],
                (group, half * N + to),
            )
        pltpu.make_async_copy(pooled.at[col, k], arrived.at[k, col], arrived_sem.at[k]).start()

    loads[0].wait()
    row = lax.broadcasted_iota(jnp.int32, (UNIT, 2 * UNIT), 1)
    place = row - 2 * lax.broadcasted_iota(jnp.int32, (UNIT, 2 * UNIT), 0)
    pair = (place >= 0) & (place < 2)
    twice = dot(
        lengths[...].astype(jnp.float32).astype(jnp.bfloat16),
        jnp.where(pair, 1.0, 0.0).astype(jnp.bfloat16),
    )
    position = lax.rem(lax.broadcasted_iota(jnp.int32, twice.shape, 1), 2).astype(jnp.float32)
    live[...] = jnp.where(twice > position, 1.0, 0.0)
    loads[1].wait()
    pool_units(0)
    to_come = 3 * (N - 1) + 1
    for e in range(OWN):
        to_come = to_come + jnp.where(score_target(e) != group, 1, 0)
    pl.semaphore_wait(barrier, to_come)
    send_pooled(0)
    pool_units(1)
    send_pooled(1)
    for load in loads[2:]:
        load.wait()

    for m in range(N):
        slot = jnp.int32(0)
        for s in range(SLOTS):
            slot = jnp.maximum(slot, jnp.where(assign_ref[0, s] == half * N + m, s, 0))
        slots[m] = slot

    turn[pl.ds(0, 16), :] = over_bias_ref[...].astype(jnp.float32)
    turn[pl.ds(16, 16), :] = out_weight_ref[...].astype(jnp.float32)
    for t in range(4):
        bias_turned[t * 4 : (t + 1) * 4, :] = turn[pl.ds(t, 4, stride=4), :]
        weight_turned[t * 4 : (t + 1) * 4, :] = turn[pl.ds(16 + t, 4, stride=4), :]

    def partial_stage(p):
        wait(arrived.at[p], arrived_sem.at[p])

        @pl.when(p + 2 < PAIRS)
        def _():
            send_pooled(p + 2)

        total = jnp.zeros((2 * WIDE, TW), jnp.float32)
        for m in range(0, N, 2):
            rows = jnp.concatenate(
                [
                    jnp.concatenate([arrived[p, m, which], arrived[p, m + 1, which]], axis=1)
                    for which in (other_half, half)
                ],
                axis=0,
            )
            weight = jnp.concatenate([first[slots[m]], first[slots[m + 1]]], axis=0)
            total = total + dot(rows, weight)
        bias = bias_first_ref[...].astype(jnp.float32)
        for q in range(2):
            k = 2 * p + q
            part_out[k] = total[q * ROWS : (q + 1) * ROWS].astype(jnp.bfloat16)
            first_pre[k] = total[WIDE + q * ROWS : WIDE + (q + 1) * ROWS] + bias

        @pl.when(p > 0)
        def _():
            wait(part_out.at[pl.ds(2 * p - 2, 2)], part_send_sem.at[p - 1])

        for q in range(2):
            k = 2 * p + q
            remote(part_out.at[k], part_in.at[k], part_send_sem.at[p], part_sem.at[k], far)

    def tower_stage(k):
        wait(part_in.at[k], part_sem.at[k])
        pre = first_pre[k] + part_in[k].astype(jnp.float32)
        first_pre[k] = pre
        act = silu(pre).astype(jnp.bfloat16)
        pre = dot(act, second[...]) + bias_second_ref[...].astype(jnp.float32)
        second_pre[k] = pre
        out = silu(pre).astype(jnp.bfloat16)
        parts = [dot(out, over[:, q * QUARTER : (q + 1) * QUARTER]) for q in range(4)]
        for v in range(N):
            head_out[k, v] = jnp.concatenate(
                [part[v * SHARE : (v + 1) * SHARE] for part in parts], axis=0
            ).astype(jnp.bfloat16)
        for d in range(1, N):
            to = turned(y, d)
            remote(
                head_out.at[k, to],
                head_in.at[k, y],
                send_sem.at[2],
                head_sem.at[k],
                (to * N + zl, local),
            )
        pltpu.make_async_copy(head_out.at[k, y], head_in.at[k, y], head_sem.at[k]).start()

    def gather_stage(k):
        wait(head_in.at[k], head_sem.at[k])
        total = head_in[k, 0].astype(jnp.float32)
        for v in range(1, N):
            total = total + head_in[k, v].astype(jnp.float32)
        for t in range(4):
            turn[t * 16 : (t + 1) * 16, :] = total[:, t * 128 : (t + 1) * 128]
        for r in range(SHARE):
            row_out[k, r] = turn[pl.ds(r, 16, stride=SHARE), :].astype(jnp.bfloat16)
        e = lax.div(k, 2)
        for r in range(SHARE):
            to = SHARE * lax.rem(k, 2) + r

            @pl.when(to != zl)
            def _():
                remote(
                    row_out.at[k, r],
                    row_in.at[e, zl],
                    send_sem.at[3],
                    row_sem.at[e],
                    (y * N + to, local),
                )

            @pl.when(to == zl)
            def _():
                pltpu.make_async_copy(row_out.at[k, r], row_in.at[e, zl], row_sem.at[e]).start()

    def loss_stage(k):
        @pl.when(lax.rem(k, 2) == side)
        def _():
            loss_row(k, lax.div(k, 2))

    def loss_row(k, e):
        wait(row_in.at[e], row_sem.at[e])
        pre = bias_turned[...]
        for v in range(N):
            pre = pre + row_in[e, v].astype(jnp.float32)
        weight = weight_turned[...]
        score = jnp.sum(
            jnp.sum(silu(pre) * weight, axis=0, keepdims=True), axis=1, keepdims=True
        )
        label = labels_ref[ROWS * k + SHARE * y + lane_row].astype(jnp.float32)
        seed = loss_scale * (jax.nn.sigmoid(score) - label)
        mine_grad[e] = (seed * weight * silu_slope(pre)).astype(jnp.bfloat16)
        for d in range(1, N):
            remote(
                mine_grad.at[e],
                line_grad.at[k, lane_row],
                send_sem.at[4],
                line_sem.at[k],
                z_peer(d),
            )
        pltpu.make_async_copy(mine_grad.at[e], line_grad.at[k, lane_row], line_sem.at[k]).start()
        score_out[e] = jnp.broadcast_to(score, (8, 128))
        target = score_target(e)

        @pl.when(target != group)
        def _():
            remote(
                score_out.at[e],
                score_in.at[lane_row],
                score_send_sem.at[e],
                score_sem.at[0],
                (target, local),
            )

        @pl.when(target == group)
        def _():
            pltpu.make_async_copy(score_out.at[e], score_in.at[lane_row], score_sem.at[0]).start()

    def spread_stage(k):
        wait(line_grad.at[k], line_sem.at[k])
        for r in range(SHARE):
            turn[r * 16 : (r + 1) * 16, :] = line_grad[k, r].astype(jnp.float32)
        for t in range(4):
            share_grad[k, :, t * 128 : (t + 1) * 128] = jnp.concatenate(
                [turn[pl.ds(t * 4 + q, SHARE, stride=16), :] for q in range(4)], axis=0
            ).astype(jnp.bfloat16)
        for d in range(1, N):
            remote(share_grad.at[k], full_grad.at[k, y], send_sem.at[5], full_sem.at[k], y_peer(d))
        pltpu.make_async_copy(share_grad.at[k], full_grad.at[k, y], full_sem.at[k]).start()

    def back_stage(k):
        wait(full_grad.at[k], full_sem.at[k])
        rows = full_grad[k].reshape(N * 16, QUARTER)
        parts = [dot_t(rows, over[:, q * QUARTER : (q + 1) * QUARTER]) for q in range(4)]
        low = lax.rem(lax.broadcasted_iota(jnp.int32, (8, TW), 0), 8) < SHARE
        sums = []
        for v in range(N):
            both = jnp.where(
                low, parts[0][v * 16 : v * 16 + 8], parts[1][v * 16 : v * 16 + 8]
            ) + jnp.where(
                low, parts[2][v * 16 + 8 : v * 16 + 16], parts[3][v * 16 + 8 : v * 16 + 16]
            )
            sums.append(both[:SHARE] + both[SHARE:])
        tower_grad = jnp.concatenate(sums, axis=0)
        second_grad = (tower_grad * silu_slope(second_pre[k])).astype(jnp.bfloat16)
        own_first_grad[k] = (
            dot_t(second_grad, second[...]) * silu_slope(first_pre[k])
        ).astype(jnp.bfloat16)
        remote(own_first_grad.at[k], far_first_grad.at[k], send_sem.at[6], far_sem.at[k], far)

    def rows_stage(p):
        pair = pl.ds(2 * p, 2)
        for q in range(2):
            wait(far_first_grad.at[2 * p + q], far_sem.at[2 * p + q])
        grad = jnp.concatenate(
            [
                own_first_grad[pair].reshape(WIDE, TW),
                far_first_grad[pair].reshape(WIDE, TW),
            ],
            axis=0,
        )
        for m in range(0, N, 2):
            weight = jnp.concatenate([first[slots[m]], first[slots[m + 1]]], axis=0)
            out = dot_t(grad, weight).astype(jnp.bfloat16)
            for v in range(2):
                table_grad[p, m + v, half] = out[:WIDE, v * E : (v + 1) * E]
                table_grad[p, m + v, other_half] = out[WIDE:, v * E : (v + 1) * E]
        span = pl.ds(pl.multiple_of(p * WIDE, WIDE), WIDE)
        for d in range(1, N):
            to = turned(col, d)
            remote(
                table_grad.at[p, to],
                grad_hbm.at[:, col, span],
                send_sem.at[7],
                grad_sem.at[0],
                (group, half * N + to),
            )
        pltpu.make_async_copy(
            table_grad.at[p, col], grad_hbm.at[:, col, span], grad_sem.at[0]
        ).start()

    def partials(p, carry):
        partial_stage(p)
        return carry

    lax.fori_loop(0, EARLY, partials, 0)

    stages = (
        (tower_stage, 0),
        (gather_stage, 4),
        (loss_stage, 8),
        (spread_stage, 12),
        (back_stage, 16),
    )

    def tick(t, carry):
        for stage, lag in stages:

            @pl.when((t >= lag) & (t < lag + CHUNKS))
            def _():
                stage(t - lag)

            if lag == 0:

                @pl.when((t < 2 * (PAIRS - EARLY)) & (lax.rem(t, 2) == 0))
                def _():
                    partial_stage(EARLY + lax.div(t, 2))

        @pl.when((t >= LAST) & (lax.rem(t - LAST, 2) == 0))
        def _():
            rows_stage(lax.div(t - LAST, 2))

        return carry

    lax.fori_loop(0, LAST + CHUNKS - 1, tick, 0)

    wait(score_in, score_sem.at[0])
    lane = lax.broadcasted_iota(jnp.int32, (8, 128), 1)
    packed = jnp.zeros((8, 128), jnp.float32)
    for i in range(OWN):
        packed = packed + jnp.where(lane == i, score_in[i], 0.0)
    scores_ref[...] = packed

    wait(pooled.at[pl.ds(0, N - 1)], send_sem.at[0])
    wait(part_out.at[pl.ds(CHUNKS - 2, 2)], part_send_sem.at[PAIRS - 1])
    wait(head_out.at[:, pl.ds(0, N - 1)], send_sem.at[2])
    wait(row_out.at[pl.ds(0, CHUNKS - 1)], send_sem.at[3])
    wait(line_grad.at[pl.ds(0, CHUNKS - 1)], send_sem.at[4])
    wait(full_grad.at[:, pl.ds(0, N - 1)], send_sem.at[5])
    wait(own_first_grad, send_sem.at[6])
    wait(table_grad.at[:, pl.ds(0, N - 1)], send_sem.at[7])
    for e in range(OWN):

        @pl.when(score_target(e) != group)
        def _():
            wait(score_out.at[e], score_send_sem.at[e])

    wait(table_grad, grad_sem.at[0])


def on_device(
    looked_rows,
    lengths,
    assign,
    labels,
    tower_first,
    bias_first,
    tower_second,
    bias_second,
    over_weight,
    over_bias,
    out_weight,
):
    batch = looked_rows.shape[1]
    block = batch // (2 * N)
    bf16, f32 = jnp.bfloat16, jnp.float32
    any_spec = pl.BlockSpec(memory_space=pl.ANY)
    vmem_spec = pl.BlockSpec(memory_space=pltpu.VMEM)
    dma = pltpu.SemaphoreType.DMA
    scores, grad = pl.pallas_call(
        kernel,
        name="tower_step",
        out_shape=(
            jax.ShapeDtypeStruct((8, 128), f32),
            jax.ShapeDtypeStruct((2, N, block, E), bf16),
        ),
        in_specs=[any_spec] * 11,
        out_specs=(vmem_spec, any_spec),
        scratch_shapes=[
            pltpu.SMEM(assign.shape, jnp.int32),
            pltpu.SMEM(labels.shape, jnp.int32),
            pltpu.VMEM(bias_first.shape, bf16),
            pltpu.VMEM(bias_second.shape, bf16),
            pltpu.VMEM((H // 128, 128), bf16),
            pltpu.VMEM((H // 128, 128), bf16),
            pltpu.VMEM((2 * batch, E), bf16),
            pltpu.VMEM((batch // UNIT, UNIT), jnp.int32),
            pltpu.VMEM((batch // UNIT, 2 * UNIT), f32),
            pltpu.VMEM((SLOTS, E, TW), bf16),
            pltpu.VMEM((TW, TW), bf16),
            pltpu.VMEM((TW, H), bf16),
            pltpu.SMEM((N,), jnp.int32),
            pltpu.VMEM((N, PAIRS, 2, WIDE, E), bf16),
            pltpu.VMEM((PAIRS, N, 2, WIDE, E), bf16),
            pltpu.VMEM((CHUNKS, ROWS, TW), bf16),
            pltpu.VMEM((CHUNKS, ROWS, TW), bf16),
            pltpu.VMEM((CHUNKS, ROWS, TW), f32),
            pltpu.VMEM((CHUNKS, ROWS, TW), f32),
            pltpu.VMEM((CHUNKS, N, 16, QUARTER), bf16),
            pltpu.VMEM((CHUNKS, N, 16, QUARTER), bf16),
            pltpu.VMEM((64, 128), f32),
            pltpu.VMEM((16, 128), f32),
            pltpu.VMEM((16, 128), f32),
            pltpu.VMEM((CHUNKS, SHARE, 16, 128), bf16),
            pltpu.VMEM((CHUNKS // 2, N, 16, 128), bf16),
            pltpu.VMEM((CHUNKS // 2, 16, 128), bf16),
            pltpu.VMEM((CHUNKS, SHARE, 16, 128), bf16),
            pltpu.VMEM((CHUNKS, 16, QUARTER), bf16),
            pltpu.VMEM((CHUNKS, N, 16, QUARTER), bf16),
            pltpu.VMEM((CHUNKS, ROWS, TW), bf16),
            pltpu.VMEM((CHUNKS, ROWS, TW), bf16),
            pltpu.VMEM((PAIRS, N, 2, WIDE, E), bf16),
            pltpu.VMEM((OWN, 8, 128), f32),
            pltpu.VMEM((OWN, 8, 128), f32),
            dma((11,)),
            dma((8,)),
            dma((PAIRS,)),
            dma((CHUNKS,)),
            dma((CHUNKS,)),
            dma((CHUNKS // 2,)),
            dma((CHUNKS,)),
            dma((CHUNKS,)),
            dma((CHUNKS,)),
            dma((1,)),
            dma((1,)),
            dma((OWN,)),
            dma((PAIRS,)),
        ],
        compiler_params=pltpu.CompilerParams(
            collective_id=0, has_side_effects=True, vmem_limit_bytes=63 * 2**20
        ),
    )(
        looked_rows.reshape(2 * batch, E),
        lengths.reshape(batch // UNIT, UNIT),
        assign,
        labels,
        tower_first.reshape(SLOTS, E, TW),
        bias_first,
        tower_second[0],
        bias_second,
        over_weight,
        over_bias.reshape(H // 128, 128),
        out_weight.reshape(H // 128, 128),
    )
    return scores[0, :OWN], grad.reshape(1, batch, E)


def solution(mesh):
    return jax.shard_map(
        on_device,
        mesh=mesh,
        in_specs=(
            P(("group", "local"), None, None, None),
            P(("group", "local"), None),
            P("group", None),
            P("local"),
            P("group", None, None),
            P("group", None),
            P("group", None, None),
            P("group", None),
            P("group", None),
            P(),
            P(),
        ),
        out_specs=(P(("local", "group")), P(("group", "local"), None, None)),
        check_vma=False,
    )
```

time: 128 us -> 120 us (0.938)
  Pallas kernels: 122 us -> 115 us
    pallas_call x1, Pallas kernels: 122 us -> 115 us  [on_device(): pl.pallas_call(kernel, name='tower_step', out_shape=(jax.ShapeDtypeStruct...]
where the time goes in v2:
time: 120 us; the launch traced here: 119 us
  Pallas kernels  115 us (96%)
  local copies, waits for them, and re-layouts  3.45 us (3%)
    pallas_call x1, Pallas kernels, on_device(): pl.pallas_call(kernel, name='tower_step', out_shape=(jax.ShapeDtypeStruct...  115 us

profile of v2, /device:TPU:1, one launch (start us, length us, event | category | flops | bytes accessed | tf_op | source)
XLA Modules:
  0.0 119.3 jit_solution(6702415035902233911)
XLA Ops:
  0.6 115.2 %tower_step.1 = (f32[8,128]{1,0:T(8,128)}, bf16[2,8,256,128]{3,2,1,0:T(8,128)(2,1)}) custom-call(bf16[8192,128]{1,0:T(8,128)(2,1)} %bitcast.9, s32[32,128]{1,0:T(8,128)} %bitcast.13, s32[1,16]{1,0:T(1,128)} %assign_hbm.1, s32[256]{0:T(256)} %labels_hbm.1, bf16[16,128,512]{2,1,0:T(8,128)(2,1)} %bitcast.10, bf16[1,512]{1,0:T(2,128)(2,1)} %bias_first_hbm.1, ...), custom_call_target="tpu_custom_call" | custom-call | tf_op jit(solution)/shard_map/tower_step/pallas_call | solution.py:507
  115.9 1.2 slice_bitcast_fusion
  117.1 2.3 %copy.14 = bf16[1,4096,128]{2,1,0:T(8,128)(2,1)} copy(bf16[1,4096,128]{2,1,0:T(8,128)(2,1)} %bitcast.11) | data formatting | bytes 2097152

commit v3 on v2

--- a/solution.py
+++ b/solution.py
@@ -395,35 +395,27 @@
         ).astype(jnp.bfloat16)
         remote(own_first_grad.at[k], far_first_grad.at[k], send_sem.at[6], far_sem.at[k], far)
 
-    def rows_stage(p):
-        pair = pl.ds(2 * p, 2)
-        for q in range(2):
-            wait(far_first_grad.at[2 * p + q], far_sem.at[2 * p + q])
-        grad = jnp.concatenate(
-            [
-                own_first_grad[pair].reshape(WIDE, TW),
-                far_first_grad[pair].reshape(WIDE, TW),
-            ],
-            axis=0,
-        )
+    def rows_stage(k):
+        wait(far_first_grad.at[k], far_sem.at[k])
+        grad = jnp.concatenate([own_first_grad[k], far_first_grad[k]], axis=0)
         for m in range(0, N, 2):
             weight = jnp.concatenate([first[slots[m]], first[slots[m + 1]]], axis=0)
             out = dot_t(grad, weight).astype(jnp.bfloat16)
             for v in range(2):
-                table_grad[p, m + v, half] = out[:WIDE, v * E : (v + 1) * E]
-                table_grad[p, m + v, other_half] = out[WIDE:, v * E : (v + 1) * E]
-        span = pl.ds(pl.multiple_of(p * WIDE, WIDE), WIDE)
+                table_grad[k, m + v, half] = out[:ROWS, v * E : (v + 1) * E]
+                table_grad[k, m + v, other_half] = out[ROWS:, v * E : (v + 1) * E]
+        span = pl.ds(pl.multiple_of(k * ROWS, ROWS), ROWS)
         for d in range(1, N):
             to = turned(col, d)
             remote(
-                table_grad.at[p, to],
+                table_grad.at[k, to],
                 grad_hbm.at[:, col, span],
                 send_sem.at[7],
                 grad_sem.at[0],
                 (group, half * N + to),
             )
         pltpu.make_async_copy(
-            table_grad.at[p, col], grad_hbm.at[:, col, span], grad_sem.at[0]
+            table_grad.at[k, col], grad_hbm.at[:, col, span], grad_sem.at[0]
         ).start()
 
     def partials(p, carry):
@@ -438,6 +430,7 @@
         (loss_stage, 8),
         (spread_stage, 12),
         (back_stage, 16),
+        (rows_stage, LAST),
     )
 
     def tick(t, carry):
@@ -453,13 +446,9 @@
                 def _():
                     partial_stage(EARLY + lax.div(t, 2))
 
-        @pl.when((t >= LAST) & (lax.rem(t - LAST, 2) == 0))
-        def _():
-            rows_stage(lax.div(t - LAST, 2))
-
         return carry
 
-    lax.fori_loop(0, LAST + CHUNKS - 1, tick, 0)
+    lax.fori_loop(0, LAST + CHUNKS, tick, 0)
 
     wait(score_in, score_sem.at[0])
     lane = lax.broadcasted_iota(jnp.int32, (8, 128), 1)
@@ -546,7 +535,7 @@
             pltpu.VMEM((CHUNKS, N, 16, QUARTER), bf16),
             pltpu.VMEM((CHUNKS, ROWS, TW), bf16),
             pltpu.VMEM((CHUNKS, ROWS, TW), bf16),
-            pltpu.VMEM((PAIRS, N, 2, WIDE, E), bf16),
+            pltpu.VMEM((CHUNKS, N, 2, ROWS, E), bf16),
             pltpu.VMEM((OWN, 8, 128), f32),
             pltpu.VMEM((OWN, 8, 128), f32),
             dma((11,)),

time: 120 us -> 119 us (level)
  no operation moved by 1% of the time
where the time goes in v3:
time: 119 us
  Pallas kernels  115 us (97%)
  local copies, waits for them, and re-layouts  3.45 us (3%)
    pallas_call x1, Pallas kernels, on_device(): pl.pallas_call(kernel, name='tower_step', out_shape=(jax.ShapeDtypeStruct...  115 us

profile of v3, /device:TPU:1, one launch (start us, length us, event | category | flops | bytes accessed | tf_op | source)
XLA Modules:
  0.0 118.8 jit_solution(14028022284636583276)
XLA Ops:
  0.6 114.8 %tower_step.1 = (f32[8,128]{1,0:T(8,128)}, bf16[2,8,256,128]{3,2,1,0:T(8,128)(2,1)}) custom-call(bf16[8192,128]{1,0:T(8,128)(2,1)} %bitcast.9, s32[32,128]{1,0:T(8,128)} %bitcast.13, s32[1,16]{1,0:T(1,128)} %assign_hbm.1, s32[256]{0:T(256)} %labels_hbm.1, bf16[16,128,512]{2,1,0:T(8,128)(2,1)} %bitcast.10, bf16[1,512]{1,0:T(2,128)(2,1)} %bias_first_hbm.1, ...), custom_call_target="tpu_custom_call" | custom-call | tf_op jit(solution)/shard_map/tower_step/pallas_call | solution.py:496
  115.4 1.2 %slice_bitcast_fusion = f32[4]{0:T(128)} fusion(f32[8,128]{1,0:T(8,128)} %get-tuple-element.4), kind=kLoop, calls=%fused_computation | loop fusion | bytes 32 | tf_op jit(solution)/shard_map/squeeze | solution.py:571
  116.6 2.3 %copy.14 = bf16[1,4096,128]{2,1,0:T(8,128)(2,1)} copy(bf16[1,4096,128]{2,1,0:T(8,128)(2,1)} %bitcast.11) | data formatting | bytes 2097152
